TPU v7x, 512 devices: a whole 4x8x8 slice. The times are simulated.
512 devices in a mesh: seg: 16 (over z, core), dev: 32 (over y, x).
Axes of the slice: x: 4, y: 8, z: 8, core: 2. Of those that a mesh axis runs over, the one named last changes fastest.
Arguments:
- positions: float32 [3, 16, 12288, 128], P(None, 'seg', 'dev'), may hold values from -6 to 6
- velocity: float32 [3, 16, 12288, 128], P(None, 'seg', 'dev'), may hold values from -6 to 6
- node_mass: bfloat16 [16, 12288, 128], P('seg', 'dev'), may hold values from 0.5 to 2
- stiffness: bfloat16 [16, 12288, 128], P('seg', 'dev'), may hold values from 0.25 to 2
- contact_patch: int32 [16, 32, 32], P('seg', 'dev'), may hold values from -1 to 2, as said below
- cross_patch: int32 [16, 32, 2], P('seg', 'dev'), may hold values from 0 to 2
Outputs:
- velocity_next: float32 [3, 16, 12288, 128], P(None, 'seg', 'dev')
Inputs may be any that keep to these rules, and one draw needn't show every extreme that they name: `contact_patch`: entry [s, i, q] is -1 where runs i and q of segment s form no contact pair, else the number within run i of run i's patch in that pair; entry [s, i, q] is -1 exactly when entry [s, q, i] is; entries [s, i, i] are -1; in every segment some run has a pair with every other run. `cross_patch`: entry [s, i, 0] is the number within run i of the patch of segment s that meets run i of the next segment; entry [s, i, 1] the one that meets run i of the previous segment.
All inputs are finite; a program needn't handle non-finite values.
Results may differ from a plain program's by a relative error of at most 0.0028.
Values may be sent and summed in bfloat16 or wider, within the bound.
A program may use at most 64 MiB of HBM per device.

v0:
```python
import math

import jax
import jax.numpy as jnp
from jax import lax
from jax.sharding import PartitionSpec as P

PATCH_ROWS = 128
BAND = 4


penalty = 1.5
reach_sq = 4.0
time_step = 0.2


def extended_2(array, sides, width):
    for axis, dim in sides:
        devices, length = (lax.axis_size(axis), array.shape[dim])
        up = [(i, (i + 1) % devices) for i in range(devices - 1)]
        down = [(j, i) for i, j in up]
        last = lax.slice_in_dim(array, length - width, length, axis=dim)
        initial = lax.slice_in_dim(array, 0, width, axis=dim)
        before = lax.ppermute(last, axis, up)
        after = lax.ppermute(initial, axis, down)
        array = jnp.concatenate([before, array, after], axis=dim)
    return array


def from_behind(block, axis, distance):
    devices = range(lax.axis_size(axis))
    route = [((i - distance) % len(devices), i) for i in devices]
    return lax.ppermute(block, axis, route)


def pair_forces(own_patch, other_patch):
    columns = own_patch.shape[-1]
    leading = [(0, 0)] * (own_patch.ndim - 1)
    padded = jnp.pad(other_patch, leading + [(BAND, BAND)])
    inside = jnp.pad(jnp.ones((columns,), jnp.float32), (BAND, BAND))
    force_own = jnp.zeros(own_patch.shape, jnp.float32)
    force_other = jnp.zeros(padded.shape, jnp.float32)
    for offset in range(2 * BAND + 1):
        facing = padded[..., offset : offset + columns]
        differ = own_patch - facing
        weight = (
            penalty
            * jnp.exp(-jnp.sum(differ * differ, axis=-3, keepdims=True) / reach_sq)
            * inside[offset : offset + columns]
        )
        pulled = weight * differ
        force_own = force_own + pulled
        force_other = force_other - jnp.pad(pulled, leading + [(offset, 2 * BAND - offset)])
    return (force_own, force_other[..., BAND : BAND + columns])


def slot_forces(own_slots, other_slots):
    total = own_slots.shape[0]
    group = math.gcd(total, 8)
    shaped = (total // group, group) + own_slots.shape[1:]

    def evaluate(blocks):
        return pair_forces(blocks[0].astype(jnp.float32), blocks[1].astype(jnp.float32))

    force_own, force_other = lax.map(
        evaluate, (own_slots.reshape(shaped), other_slots.reshape(shaped))
    )
    return (force_own.reshape(own_slots.shape), force_other.reshape(own_slots.shape))


def spread_slots(slot_index, slot_live, slot_values, count):
    patch_ids = jnp.arange(count, dtype=jnp.int32)
    weights = ((slot_index[:, None] == patch_ids[None, :]) & slot_live[:, None]).astype(jnp.float32)
    return jnp.einsum("qp,qcrk->cprk", weights, slot_values, precision=lax.Precision.HIGHEST)


def shards(positions, velocity, node_mass, stiffness, contact_patch, cross_patch):
    runs = lax.axis_size("dev")
    me_index = lax.axis_index("dev")
    places = positions[:, 0]
    rows = places.shape[1]
    columns = places.shape[2]
    count = rows // PATCH_ROWS
    springs = stiffness[0].astype(jnp.float32)
    stacked = jnp.concatenate([places, springs[None]], axis=0)
    extended = extended_2(stacked, (("dev", 1),), 1)
    ext_places = extended[:3]
    ext_springs = extended[3]
    edges = jnp.arange(rows + 1)
    keep = jnp.where(
        (edges == 0) & (me_index == 0) | (edges == rows) & (me_index == runs - 1), 0.0, 1.0
    ).astype(jnp.float32)
    row_flow = (
        0.5
        * (ext_springs[1:] + ext_springs[:-1])
        * keep[:, None]
        * (ext_places[:, 1:] - ext_places[:, :-1])
    )
    internal = row_flow[:, 1:] - row_flow[:, :-1]
    col_flow = 0.5 * (springs[:, 1:] + springs[:, :-1]) * (places[..., 1:] - places[..., :-1])
    still = (0, 0)
    internal = (
        internal
        + jnp.pad(col_flow, (still, still, (0, 1)))
        - jnp.pad(col_flow, (still, still, (1, 0)))
    )
    rounded = lax.optimization_barrier(places.astype(jnp.bfloat16))
    patches = jnp.transpose(rounded.reshape(3, count, PATCH_ROWS, columns), (1, 0, 2, 3))
    table = contact_patch[0, 0]
    linked = table >= 0
    chosen = jnp.maximum(table, 0)
    facing_next = cross_patch[0, 0, 0]
    facing_prev = cross_patch[0, 0, 1]
    next_patch = lax.dynamic_index_in_dim(patches, facing_next, 0, keepdims=False)
    prev_patch = lax.dynamic_index_in_dim(patches, facing_prev, 0, keepdims=False)
    from_next = from_behind(prev_patch, "seg", -1)
    seg_own, seg_back = pair_forces(next_patch.astype(jnp.float32), from_next.astype(jnp.float32))
    slot_patches = jnp.take(patches, chosen, axis=0)
    outgoing = jnp.where(linked[:, None, None, None], slot_patches, jnp.zeros_like(slot_patches))
    incoming = lax.all_to_all(outgoing, "dev", split_axis=0, concat_axis=0, tiled=True)
    force_own, force_back = slot_forces(slot_patches, incoming)
    contact = spread_slots(chosen, linked, force_own, count)
    from_prev = from_behind(next_patch, "seg", 1)
    seg_prev, seg_unused = pair_forces(
        prev_patch.astype(jnp.float32), from_prev.astype(jnp.float32)
    )
    patch_ids = jnp.arange(count, dtype=jnp.int32)
    at_next = (patch_ids == facing_next).astype(jnp.float32)[None, :, None, None]
    at_prev = (patch_ids == facing_prev).astype(jnp.float32)[None, :, None, None]
    contact = contact + at_next * seg_own[:, None] + at_prev * seg_prev[:, None]
    force = internal + contact.reshape(3, rows, columns)
    moved = velocity[:, 0] + time_step * force / node_mass[0].astype(jnp.float32)
    return moved[:, None]


def solution(mesh):
    return jax.shard_map(
        shards,
        mesh=mesh,
        in_specs=(
            P(None, "seg", "dev", None),
            P(None, "seg", "dev", None),
            P("seg", "dev", None),
            P("seg", "dev", None),
            P("seg", "dev", None),
            P("seg", "dev", None),
        ),
        out_specs=P(None, "seg", "dev", None),
        check_vma=False,
    )
```

profile of v0, /device:TPU:24, one launch (start us, length us, event | category | flops | bytes accessed | tf_op | source)
XLA Modules:
  0.0 160.0 jit_solution(14670952766575089777)
XLA Ops:
  2.0 1.1 bitcast_convert_fusion.2
  3.1 1.2 gather_fusion
  4.3 2.4 %select_select_fusion = bf16[32,3,128,128]{3,2,1,0:T(8,128)(2,1)} fusion(bf16[32,3,128,128]{3,2,1,0:T(8,128)(2,1)S(1)} %gather_fusion, pred[32]{0:T(512)(128)(4,1)S(1)} %broadcast_compare_fusion, pred[32]{0:T(512)(128)(4,1)S(1)} %get-tuple-element.141), kind=kLoop, calls=%fused_computation.57 | loop fusion | flops 3145728 | bytes 6291520 | tf_op jit(solution)/shard_map/jit(_where)/select_n | solution.py:119
  7.0 10.1 %all-to-all-start = ((bf16[32,3,128,128]{3,2,1,0:T(8,128)(2,1)}), bf16[32,3,128,128]{3,2,1,0:T(8,128)(2,1)S(1)}, u32[]{:S(2)}, u32[]{:S(2)}) async-start(bf16[32,3,128,128]{3,2,1,0:T(8,128)(2,1)} %select_select_fusion), calls=%async_computation | async-start | bytes 6291456 | tf_op jit(solution)/shard_map/all_to_all | solution.py:120
  20.2 7.9 %collective-permute-start.2 = (bf16[3,128,128]{2,1,0:T(8,128)(2,1)}, bf16[3,128,128]{2,1,0:T(8,128)(2,1)S(1)}, u32[]{:S(2)}, u32[]{:S(2)}) collective-permute-start(bf16[3,128,128]{2,1,0:T(8,128)(2,1)} %dynamic-slice_bitcast_fusion), channel_id=1, source_target_pairs={{32,0},{64,32},{96,64},{128,96},{160,128},{192,160},{224,192},{256... | collective-permute-start | bytes 294920 | tf_op jit(solution)/shard_map/ppermute | solution.py:33
  28.1 1.6 convert_bitcast_fusion
  30.4 1.3 pad_maximum_fusion.5
  31.7 4.6 %collective-permute-start = (f32[4,1,128]{2,1,0:T(1,128)}, f32[4,1,128]{2,1,0:T(1,128)S(1)}, u32[]{:S(2)}, u32[]{:S(2)}) collective-permute-start(f32[4,1,128]{2,1,0:T(1,128)} %get-tuple-element.111), channel_id=1, source_target_pairs={{1,0},{2,1},{3,2},{4,3},{5,4},{6,5},{7,6},{8,7},{9,8},{10,9},{11,1... | collective-permute-start | bytes 6152 | tf_op jit(solution)/shard_map/ppermute | solution.py:25
  36.3 1.9 %collective-permute-start.1 = (f32[4,1,128]{2,1,0:T(1,128)S(1)}, f32[4,1,128]{2,1,0:T(1,128)S(1)}, u32[]{:S(2)}, u32[]{:S(2)}) collective-permute-start(f32[4,1,128]{2,1,0:T(1,128)S(1)} %get-tuple-element.112), channel_id=1, source_target_pairs={{0,1},{1,2},{2,3},{3,4},{4,5},{5,6},{6,7},{7,8},{8,9},{9,10},{10,1... | collective-permute-start | bytes 6152 | tf_op jit(solution)/shard_map/ppermute | solution.py:24
  39.5 1.6 bitcast_convert_fusion.1
  41.1 1.1 fusion.30
  42.3 1.0 fusion.21
  43.3 4.0 %broadcast_select_fusion = bf16[4,8,3,128,128]{4,3,2,1,0:T(8,128)(2,1)} fusion(bf16[4,8,3,128,128]{4,3,2,1,0:T(8,128)(2,1)} %bitcast.82, pred[4,8]{1,0:T(4,128)(4,1)S(1)} %copy-done.23), kind=kLoop, calls=%fused_computation.58 | loop fusion | flops 1572864 | bytes 6291488 | tf_op jit(solution)/shard_map/jit(_take)/select_n | solution.py:118
  47.3 1.8 %compare_convert_fusion = (f32[3]{0:T(128)}, f32[3]{0:T(128)}) fusion(s32[]{:T(128)} %bitcast.21, s32[]{:T(128)} %bitcast.19), kind=kLoop, calls=%fused_computation.178 | loop fusion | flops 12 | bytes 32 | tf_op jit(solution)/shard_map/convert_element_type | solution.py:129
  50.8 31.8 %collective-permute-done = f32[4,1,128]{2,1,0:T(1,128)S(1)} collective-permute-done((f32[4,1,128]{2,1,0:T(1,128)}, f32[4,1,128]{2,1,0:T(1,128)S(1)}, u32[]{:S(2)}, u32[]{:S(2)}) %collective-permute-start) | collective-permute-done | bytes 2080 | tf_op jit(solution)/shard_map/ppermute | solution.py:25
  82.6 4.8 %collective-permute-done.1 = f32[4,1,128]{2,1,0:T(1,128)S(1)} collective-permute-done((f32[4,1,128]{2,1,0:T(1,128)S(1)}, f32[4,1,128]{2,1,0:T(1,128)S(1)}, u32[]{:S(2)}, u32[]{:S(2)}) %collective-permute-start.1) | collective-permute-done | bytes 2080 | tf_op jit(solution)/shard_map/ppermute | solution.py:24
  87.4 1.1 fusion.29
  88.5 2.2 %fusion.20 = f32[3,385,128]{2,1,0:T(8,128)} fusion(f32[4,1,128]{2,1,0:T(1,128)S(1)} %collective-permute-done.1, f32[1,384,128]{2,1,0:T(8,128)} %copy-done.3, f32[3,384,128]{2,1,0:T(8,128)} %bitcast.85, f32[4,1,128]{2,1,0:T(1,128)S(1)} %collective-permute-done, f32[385,128]{1,0:T(8,128)S(1)} %fusion.29), kind=kLoop, calls=%fused_computation.80 | loop fusion | flops 887040 | bytes 1579008 | tf_op jit(solution)/shard_map/mul | solution.py:94
  91.3 10.4 %collective-permute-done.3 = bf16[3,128,128]{2,1,0:T(8,128)(2,1)S(1)} collective-permute-done((bf16[3,128,128]{2,1,0:T(8,128)(2,1)S(1)}, bf16[3,128,128]{2,1,0:T(8,128)(2,1)S(1)}, u32[]{:S(2)}, u32[]{:S(2)}) %collective-permute-start.3) | collective-permute-done | bytes 98336 | tf_op jit(solution)/shard_map/ppermute | solution.py:33
  102.6 1.2 multiply_add_fusion
  103.7 1.2 multiply_add_fusion.1
  104.9 44.3 %while.12 = (s32[]{:T(128)}, f32[4,8,3,128,128]{4,3,2,1,0:T(8,128)}, bf16[4,8,3,128,128]{4,3,2,1,0:T(8,128)(2,1)}, bf16[4,8,3,128,128]{4,3,2,1,0:T(8,128)(2,1)S(1)}, s32[]{:T(128)}, /*index=5*/f32[]{:T(128)}) while((s32[]{:T(128)}, f32[4,8,3,128,128]{4,3,2,1,0:T(8,128)}, bf16[4,8,3,128,128]{4,3,2,1,0:T(8,128)(2,1)}, ...), condition=%wide.region_10.11_spmd, body=%wide.region_0.10_spmd.sunk | while | flops 24773632 | bytes 28321360 | solution.py:65
  105.3 4.7 %multiply_reduce_fusion.28 = (f32[8,128,128]{2,1,0:T(8,128)S(1)}, f32[8,128,128]{2,1,0:T(8,128)S(1)}, f32[8,128,128]{2,1,0:T(8,128)S(1)}, f32[8,128,128]{2,1,0:T...) fusion(f32[8,3,128,128]{3,2,1,0:T(8,128)S(1)} %bitcast_convert_, ...), kind=kLoop, calls=%fused_computation.27.clone.1 | loop fusion | flops 10223616 | bytes 7864324 | tf_op jit(solution)/shard_map/while/body/eval_jaxpr/reduce_sum | solution.py:48
  110.8 5.4 %bitcast_dynamic-update-slice_fusion.2 = f32[4,8,3,128,128]{4,3,2,1,0:T(8,128)} fusion(f32[4,8,3,128,128]{4,3,2,1,0:T(8,128)} %get-tuple-element.235, s32[]{:T(128)} %get-tuple-element.234, f32[8,3,128,128]{3,2,1,0:T(8,128)S(1)} %bitcast_convert_fusion.4, f32[8,128,128]{2,1,0:T(8,128)S(1)} %get-tuple-element.207, ...), kind=kLoop, calls=%fused_computation.18.clone.1 | loop fusion | flops 10616832 | bytes 8651264 | tf_op jit(solution)/shard_map/while/body/jit(dynamic_update_index_in_dim)/dynamic_update_slice | solution.py:65
  116.3 4.7 %multiply_reduce_fusion.28 = (f32[8,128,128]{2,1,0:T(8,128)S(1)}, f32[8,128,128]{2,1,0:T(8,128)S(1)}, f32[8,128,128]{2,1,0:T(8,128)S(1)}, f32[8,128,128]{2,1,0:T...) fusion(f32[8,3,128,128]{3,2,1,0:T(8,128)S(1)} %bitcast_convert_, ...), kind=kLoop, calls=%fused_computation.27.clone.1 | loop fusion | flops 10223616 | bytes 7864324 | tf_op jit(solution)/shard_map/while/body/eval_jaxpr/reduce_sum | solution.py:48
  121.9 5.3 %bitcast_dynamic-update-slice_fusion.2 = f32[4,8,3,128,128]{4,3,2,1,0:T(8,128)} fusion(f32[4,8,3,128,128]{4,3,2,1,0:T(8,128)} %get-tuple-element.235, s32[]{:T(128)} %get-tuple-element.234, f32[8,3,128,128]{3,2,1,0:T(8,128)S(1)} %bitcast_convert_fusion.4, f32[8,128,128]{2,1,0:T(8,128)S(1)} %get-tuple-element.207, ...), kind=kLoop, calls=%fused_computation.18.clone.1 | loop fusion | flops 10616832 | bytes 8651264 | tf_op jit(solution)/shard_map/while/body/jit(dynamic_update_index_in_dim)/dynamic_update_slice | solution.py:65
  127.4 4.7 %multiply_reduce_fusion.28 = (f32[8,128,128]{2,1,0:T(8,128)S(1)}, f32[8,128,128]{2,1,0:T(8,128)S(1)}, f32[8,128,128]{2,1,0:T(8,128)S(1)}, f32[8,128,128]{2,1,0:T...) fusion(f32[8,3,128,128]{3,2,1,0:T(8,128)S(1)} %bitcast_convert_, ...), kind=kLoop, calls=%fused_computation.27.clone.1 | loop fusion | flops 10223616 | bytes 7864324 | tf_op jit(solution)/shard_map/while/body/eval_jaxpr/reduce_sum | solution.py:48
  132.9 5.3 %bitcast_dynamic-update-slice_fusion.2 = f32[4,8,3,128,128]{4,3,2,1,0:T(8,128)} fusion(f32[4,8,3,128,128]{4,3,2,1,0:T(8,128)} %get-tuple-element.235, s32[]{:T(128)} %get-tuple-element.234, f32[8,3,128,128]{3,2,1,0:T(8,128)S(1)} %bitcast_convert_fusion.4, f32[8,128,128]{2,1,0:T(8,128)S(1)} %get-tuple-element.207, ...), kind=kLoop, calls=%fused_computation.18.clone.1 | loop fusion | flops 10616832 | bytes 8651264 | tf_op jit(solution)/shard_map/while/body/jit(dynamic_update_index_in_dim)/dynamic_update_slice | solution.py:65
  138.4 4.7 %multiply_reduce_fusion.28 = (f32[8,128,128]{2,1,0:T(8,128)S(1)}, f32[8,128,128]{2,1,0:T(8,128)S(1)}, f32[8,128,128]{2,1,0:T(8,128)S(1)}, f32[8,128,128]{2,1,0:T...) fusion(f32[8,3,128,128]{3,2,1,0:T(8,128)S(1)} %bitcast_convert_, ...), kind=kLoop, calls=%fused_computation.27.clone.1 | loop fusion | flops 10223616 | bytes 7864324 | tf_op jit(solution)/shard_map/while/body/eval_jaxpr/reduce_sum | solution.py:48
  143.9 5.3 %bitcast_dynamic-update-slice_fusion.2 = f32[4,8,3,128,128]{4,3,2,1,0:T(8,128)} fusion(f32[4,8,3,128,128]{4,3,2,1,0:T(8,128)} %get-tuple-element.235, s32[]{:T(128)} %get-tuple-element.234, f32[8,3,128,128]{3,2,1,0:T(8,128)S(1)} %bitcast_convert_fusion.4, f32[8,128,128]{2,1,0:T(8,128)S(1)} %get-tuple-element.207, ...), kind=kLoop, calls=%fused_computation.18.clone.1 | loop fusion | flops 10616832 | bytes 8651264 | tf_op jit(solution)/shard_map/while/body/jit(dynamic_update_index_in_dim)/dynamic_update_slice | solution.py:65
  149.3 8.4 %fusion.16 = f32[3,3,128,128]{3,1,2,0:T(4,128)S(1)} fusion(f32[32,3,128,128]{3,2,1,0:T(8,128)} %bitcast.15, f32[3,128,128]{2,1,0:T(8,128)S(1)} %copy-done.6, f32[3]{0:T(128)S(1)} %copy-done.10, f32[3,128,128]{2,1,0:T(8,128)} %multiply_add_fusion.1, f32[3]{0:T(128)S(1)} %copy-done.11, s32[32]{0:T(128)S(1)} %copy-done.9, pred[32]{0:T(512)(128)(4,1)S(1)} %copy-done.22), kind=kOutput, calls=%fused_computation.61 | convolution fusion | flops 57213120 | bytes 7274680 | tf_op jit(solution)/shard_map/qp,qcrk->cprk/dot_general | solution.py:74
  158.9 1.1 fusion.27
  (105 shorter events, 11.6 us)
Async XLA Ops:
  0.7 2.5 %copy-start.8 = (s32[32]{0:T(128)}, s32[32]{0:T(128)S(1)}, u32[]{:S(2)}) copy-start(s32[32]{0:T(128)S(1)} %maximum_bitcast_fusion) | copy-start | bytes 388
  1.3 3.0 %copy-start.21 = (pred[32]{0:T(512)(128)(4,1)}, pred[32]{0:T(512)(128)(4,1)S(1)}, u32[]{:S(2)}) copy-start(pred[32]{0:T(512)(128)(4,1)S(1)} %get-tuple-element.141) | copy-start | bytes 100
  4.3 2.7 %copy-start = (bf16[32,3,128,128]{3,2,1,0:T(8,128)(2,1)}, bf16[32,3,128,128]{3,2,1,0:T(8,128)(2,1)S(1)}, u32[]{:S(2)}) copy-start(bf16[32,3,128,128]{3,2,1,0:T(8,128)(2,1)S(1)} %gather_fusion) | copy-start | bytes 9437188
  7.0 10.1 %copy-start.12 = (s32[1,1,2]{2,1,0:T(1,128)S(1)}, s32[1,1,2]{2,1,0:T(1,128)}, u32[]{:S(2)}) copy-start(s32[1,1,2]{2,1,0:T(1,128)} %param.13) | copy-start | bytes 28
  7.0 97.9 %all-to-all-start = ((bf16[32,3,128,128]{3,2,1,0:T(8,128)(2,1)}), bf16[32,3,128,128]{3,2,1,0:T(8,128)(2,1)S(1)}, u32[]{:S(2)}, u32[]{:S(2)}) async-start(bf16[32,3,128,128]{3,2,1,0:T(8,128)(2,1)} %select_select_fusion), calls=%async_computation | async-start | bytes 6291456 | tf_op jit(solution)/shard_map/all_to_all | solution.py:120
  20.2 70.5 %collective-permute-start.2 = (bf16[3,128,128]{2,1,0:T(8,128)(2,1)}, bf16[3,128,128]{2,1,0:T(8,128)(2,1)S(1)}, u32[]{:S(2)}, u32[]{:S(2)}) collective-permute-start(bf16[3,128,128]{2,1,0:T(8,128)(2,1)} %dynamic-slice_bitcast_fusion), channel_id=1, source_target_pairs={{32,0},{64,32},{96,64},{128,96},{160,128},{192,160},{224,192},{256... | collective-permute-start | bytes 294920 | tf_op jit(solution)/shard_map/ppermute | solution.py:33
  29.7 0.7 copy-start.3
  31.7 50.9 %collective-permute-start = (f32[4,1,128]{2,1,0:T(1,128)}, f32[4,1,128]{2,1,0:T(1,128)S(1)}, u32[]{:S(2)}, u32[]{:S(2)}) collective-permute-start(f32[4,1,128]{2,1,0:T(1,128)} %get-tuple-element.111), channel_id=1, source_target_pairs={{1,0},{2,1},{3,2},{4,3},{5,4},{6,5},{7,6},{8,7},{9,8},{10,9},{11,1... | collective-permute-start | bytes 6152 | tf_op jit(solution)/shard_map/ppermute | solution.py:25
  36.3 51.1 %collective-permute-start.1 = (f32[4,1,128]{2,1,0:T(1,128)S(1)}, f32[4,1,128]{2,1,0:T(1,128)S(1)}, u32[]{:S(2)}, u32[]{:S(2)}) collective-permute-start(f32[4,1,128]{2,1,0:T(1,128)S(1)} %get-tuple-element.112), channel_id=1, source_target_pairs={{0,1},{1,2},{2,3},{3,4},{4,5},{5,6},{6,7},{7,8},{8,9},{9,10},{10,1... | collective-permute-start | bytes 6152 | tf_op jit(solution)/shard_map/ppermute | solution.py:24
  38.8 3.4 %copy-start.1 = (f32[3,1,384,128]{3,2,1,0:T(8,128)S(1)}, f32[3,1,384,128]{3,2,1,0:T(8,128)}, u32[]{:S(2)}) copy-start(f32[3,1,384,128]{3,2,1,0:T(8,128)} %param.8) | copy-start | bytes 1769476
  38.8 4.5 %copy-start.23 = (pred[4,8]{1,0:T(4,128)(4,1)S(1)}, pred[4,8]{1,0:T(4,128)(4,1)}, u32[]{:S(2)}) copy-start(pred[4,8]{1,0:T(4,128)(4,1)} %le.21) | copy-start | bytes 100
  90.7 11.6 %copy-start.19 = (f32[128]{0:T(128)S(1)}, f32[128]{0:T(128)}, u32[]{:S(2)}) copy-start(f32[128]{0:T(128)} %get-tuple-element.131) | copy-start | bytes 1540
  90.7 11.6 %copy-start.20 = (f32[128]{0:T(128)S(1)}, f32[128]{0:T(128)}, u32[]{:S(2)}) copy-start(f32[128]{0:T(128)} %get-tuple-element.132) | copy-start | bytes 1540
  90.7 11.6 %copy-start.17 = (f32[128]{0:T(128)S(1)}, f32[128]{0:T(128)}, u32[]{:S(2)}) copy-start(f32[128]{0:T(128)} %get-tuple-element.133) | copy-start | bytes 1540
  90.7 11.6 %copy-start.18 = (f32[128]{0:T(128)S(1)}, f32[128]{0:T(128)}, u32[]{:S(2)}) copy-start(f32[128]{0:T(128)} %get-tuple-element.134) | copy-start | bytes 1540
  91.2 11.2 %copy-start.15 = (f32[128]{0:T(128)S(1)}, f32[128]{0:T(128)}, u32[]{:S(2)}) copy-start(f32[128]{0:T(128)} %get-tuple-element.135) | copy-start | bytes 1540
  91.2 11.2 %copy-start.16 = (f32[128]{0:T(128)S(1)}, f32[128]{0:T(128)}, u32[]{:S(2)}) copy-start(f32[128]{0:T(128)} %get-tuple-element.136) | copy-start | bytes 1540
  91.2 10.5 %collective-permute-start.3 = (bf16[3,128,128]{2,1,0:T(8,128)(2,1)S(1)}, bf16[3,128,128]{2,1,0:T(8,128)(2,1)S(1)}, u32[]{:S(2)}, u32[]{:S(2)}) collective-permute-start(bf16[3,128,128]{2,1,0:T(8,128)(2,1)S(1)} %get-tuple-element.94), channel_id=1, source_target_pairs={{480,0},{0,32},{32,64},{64,96},{96,128},{128,160},{160,192},{192,2... | collective-permute-start | bytes 294920 | tf_op jit(solution)/shard_map/ppermute | solution.py:33
  91.3 11.2 %copy-start.13 = (f32[128]{0:T(128)S(1)}, f32[128]{0:T(128)}, u32[]{:S(2)}) copy-start(f32[128]{0:T(128)} %get-tuple-element.137) | copy-start | bytes 1540
  91.3 11.2 %copy-start.14 = (f32[128]{0:T(128)S(1)}, f32[128]{0:T(128)}, u32[]{:S(2)}) copy-start(f32[128]{0:T(128)} %get-tuple-element.138) | copy-start | bytes 1540
  104.9 44.3 %copy-start.6 = (f32[3,128,128]{2,1,0:T(8,128)S(1)}, f32[3,128,128]{2,1,0:T(8,128)}, u32[]{:S(2)}) copy-start(f32[3,128,128]{2,1,0:T(8,128)} %multiply_add_fusion) | copy-start | bytes 589828
  104.9 44.3 %copy-start.9 = (s32[32]{0:T(128)S(1)}, s32[32]{0:T(128)}, u32[]{:S(2)}) copy-start(s32[32]{0:T(128)} %copy-done.8) | copy-start | bytes 388
  104.9 44.3 %copy-start.10 = (f32[3]{0:T(128)S(1)}, f32[3]{0:T(128)}, u32[]{:S(2)}) copy-start(f32[3]{0:T(128)} %get-tuple-element.151) | copy-start | bytes 40
  104.9 44.3 %copy-start.11 = (f32[3]{0:T(128)S(1)}, f32[3]{0:T(128)}, u32[]{:S(2)}) copy-start(f32[3]{0:T(128)} %get-tuple-element.152) | copy-start | bytes 40
  104.9 44.3 %copy-start.22 = (pred[32]{0:T(512)(128)(4,1)S(1)}, pred[32]{0:T(512)(128)(4,1)}, u32[]{:S(2)}) copy-start(pred[32]{0:T(512)(128)(4,1)} %copy-done.21) | copy-start | bytes 100
  149.3 8.5 %copy-start.5 = (f32[384,128]{1,0:T(8,128)S(1)}, f32[384,128]{1,0:T(8,128)}, u32[]{:S(2)}) copy-start(f32[384,128]{1,0:T(8,128)} %bitcast_convert_fusion.1) | copy-start | bytes 589828
  149.3 8.5 %copy-start.7 = (f32[3,1,384,128]{3,2,1,0:T(8,128)S(1)}, f32[3,1,384,128]{3,2,1,0:T(8,128)}, u32[]{:S(2)}) copy-start(f32[3,1,384,128]{3,2,1,0:T(8,128)} %param.9) | copy-start | bytes 1769476
  157.7 1.1 copy-start.2
  157.7 1.2 copy-start.4
where the time goes:
time: 161 us; the launch traced here: 160 us
  other arithmetic  70.4 us (44%)
  waiting for transfers between devices  47.1 us (29%)
  starting transfers between devices  24.5 us (15%)
  matrix products  8.37 us (5%)
  local copies, waits for them, and re-layouts  5.24 us (3%)
  between operations  4.03 us (3%)
    ppermute x1, waiting for transfers between devices, extended_2(): after = lax.ppermute(initial, axis, down)  31.8 us
    dynamic_update_slice x4, other arithmetic, slot_forces(): lax.map(evaluate, (own_slots.reshape(shaped), other_slots.reshape(shaped)))  21.3 us
    reduce_sum x6, other arithmetic, pair_forces(): jnp.sum(differ * differ, axis=-3, keepdims=True)  19.9 us
    ppermute x2, waiting for transfers between devices, from_behind(): return lax.ppermute(block, axis, route)  10.4 us
    all_to_all x1, starting transfers between devices, shards(): lax.all_to_all(outgoing, 'dev', split_axis=0, concat_axis=0, tiled=True)  10.1 us
    dot_general x1, matrix products, spread_slots(): jnp.einsum('qp,qcrk->cprk', weights, slot_values, precision=lax.Precision...  8.37 us
    ppermute x2, starting transfers between devices, from_behind(): return lax.ppermute(block, axis, route)  7.94 us
    ppermute x1, waiting for transfers between devices, extended_2(): before = lax.ppermute(last, axis, up)  4.77 us
  transfers between devices with their start and end apart: 5, of which 3 were waited for; matrix products, arithmetic and copies ran while one was open for 14% of the time, Pallas kernels for 0%

commit v1 on v0

v1 whole, which is shorter than its diff:
```python
import functools
import math

import jax
import jax.numpy as jnp
from jax import lax
from jax.experimental import pallas as pl
from jax.experimental.pallas import tpu as pltpu
from jax.sharding import PartitionSpec as P

RUNS = 32
XS = 4
YS = 8
PATCHES = 3
N = 128
BAND = 4
PAD = 8
STRIDE = 4
WINDOW = 8 * STRIDE
ROWS = PATCHES * N

penalty = 1.5
reach_sq = 4.0
time_step = 0.2
K = math.log2(math.e) / reach_sq
FAR = -1.0e4

CHUNKS = ((0, 80, (0, 1)), (80, 128, (2, 3)))
OPPOSITE = (((0, 48), (48, 80)), ((80, 96), (96, 128)))
HALVES = OPPOSITE

TWO, RIGHT, LEFT, OWN = range(4)
COPIES = 160


class Copies:
    def __init__(self, send_sem, recv_sem):
        self.send_sem, self.recv_sem = send_sem, recv_sem
        self.made = {}

    def start(self, name, src, dst, device):
        n = len(self.made)
        copy = pltpu.make_async_remote_copy(
            src_ref=src,
            dst_ref=dst,
            send_sem=self.send_sem.at[n],
            recv_sem=self.recv_sem.at[n],
            device_id=device,
            device_id_type=pl.DeviceIdType.MESH,
        )
        copy.start()
        self.made[name] = copy

    def arrived(self, name):
        self.made[name].wait_recv()

    def sent(self):
        for copy in self.made.values():
            copy.wait_send()


def kernel(
    table, cross, pos, vel, mass, stiff, out,
    place, mass_v, stiff_v, spring, share, own, y_land, x_land, src, tgt, acc,
    ship, raw, done, force, z_send, z_land, h_send, h_land,
    tab_y1, tab_y2, tab_y3, tab_y4, tab_y5, tab_y6, tab_y7, tab_x1, tab_x2, tab_x3, pick,
    local_sem, send_sem, recv_sem,
):
    seg = lax.axis_index("seg")
    dev = lax.axis_index("dev")
    segs = lax.axis_size("seg")
    y = dev // XS
    x = dev % XS

    def at(dy, dx):
        return (seg, lax.rem(y + dy, YS) * XS + lax.rem(x + dx, XS))

    up, down = at(1, 0), at(YS - 1, 0)
    right, left = at(0, 1), at(0, XS - 1)
    seg_next, seg_prev = (lax.rem(seg + 1, segs), dev), (lax.rem(seg + segs - 1, segs), dev)
    dev_next, dev_prev = (seg, lax.rem(dev + 1, RUNS)), (seg, lax.rem(dev + RUNS - 1, RUNS))

    barrier = pltpu.get_barrier_semaphore()
    peers = (up, down, right, left, seg_next, seg_prev, dev_next, dev_prev)
    for peer in peers:
        pl.semaphore_signal(barrier, inc=1, device_id=peer, device_id_type=pl.DeviceIdType.MESH)

    loads = []
    for p in range(PATCHES):
        loads.append(
            pltpu.make_async_copy(
                pos.at[:, 0, pl.ds(p * N, N), :],
                place.at[:, pl.ds(PAD + p * N, N), :],
                local_sem.at[p],
            )
        )
    loads.append(pltpu.make_async_copy(stiff.at[0], stiff_v, local_sem.at[3]))
    loads.append(pltpu.make_async_copy(mass.at[0], mass_v, local_sem.at[4]))
    loads.append(pltpu.make_async_copy(vel, out, local_sem.at[5]))
    for load in loads:
        load.start()

    def clear(n, carry):
        for c in range(4):
            edge = jnp.full((PAD, N), FAR if c == 3 else 0.0, jnp.float32)
            src[n, c, pl.ds(0, PAD), :] = edge
            src[n, c, pl.ds(PAD + N, PAD), :] = edge
        return carry

    lax.fori_loop(0, 8 * PATCHES + 2, clear, 0)

    copies = Copies(send_sem, recv_sem)

    def columns(k):
        lo, hi, _ = CHUNKS[k]
        return pl.ds(lo, hi - lo)

    def beta(xs):
        return -K * (xs[0] * xs[0] + xs[1] * xs[1] + xs[2] * xs[2])

    entered = False
    for p in range(PATCHES):
        loads[p].wait()
        parts = []
        for c in range(3):
            turned = place[c, pl.ds(PAD + p * N, N), :].T.astype(jnp.bfloat16)
            own[p, c] = turned
            parts.append(turned.astype(jnp.float32))
        for c in range(3):
            src[p, c, pl.ds(PAD, N), :] = parts[c]
            tgt[OWN * PATCHES + p, c] = parts[c] * (2 * K)
        src[p, 3, pl.ds(PAD, N), :] = beta(parts)
        if not entered:
            pl.semaphore_wait(barrier, len(peers))
            entered = True
        part = own.at[p, :, columns(0), :]
        copies.start(("y", 1, 0, p), part, y_land.at[0, p, :, columns(0), :], up)
        copies.start(("y", -1, 0, p), part, y_land.at[3, p, :, columns(0), :], down)
        copies.start(("x", 1, 0, p), part, x_land.at[LEFT, p, :, columns(0), :], right)
        copies.start(("x", -1, 0, p), part, x_land.at[RIGHT, p, :, columns(0), :], left)
    tabs_y = (table, tab_y1, tab_y2, tab_y3, tab_y4, tab_y5, tab_y6, tab_y7)
    copies.start(("ty", 1), table, tab_y1, up)
    copies.start(("ty", -1), table, tab_y4, down)
    copies.start(("tx", 1), table, tab_x3, right)
    copies.start(("tx", -1), table, tab_x2, left)
    for p in range(PATCHES):
        part = own.at[p, :, columns(1), :]
        copies.start(("y", 1, 1, p), part, y_land.at[0, p, :, columns(1), :], up)
        copies.start(("y", -1, 1, p), part, y_land.at[3, p, :, columns(1), :], down)
    meets = [cross[0, 0], cross[0, 1]]
    for c in range(3):
        z_send[0, c] = own[meets[0], c]
        z_send[1, c] = own[meets[1], c]
    copies.start(("z", 1), z_send.at[0], z_land.at[1], seg_next)
    copies.start(("z", -1), z_send.at[1], z_land.at[0], seg_prev)

    loads[3].wait()
    for b in range(ROWS // WINDOW):
        spring[pl.ds(PAD + b * WINDOW, WINDOW), :] = stiff_v[pl.ds(b * WINDOW, WINDOW), :].astype(jnp.float32)
    for e, row in enumerate((PAD, PAD + ROWS - 1)):
        for c in range(3):
            h_send[e, pl.ds(c, 1), :] = place[c, pl.ds(row, 1), :]
        h_send[e, pl.ds(3, 1), :] = spring[pl.ds(row, 1), :]
        h_send[e, pl.ds(4, 4), :] = jnp.zeros((4, N), jnp.float32)
    copies.start(("h", -1), h_send.at[0], h_land.at[1], dev_prev)
    copies.start(("h", 1), h_send.at[1], h_land.at[0], dev_next)

    def clear_sums(n, carry):
        for c in range(4):
            acc[n, c] = jnp.zeros((N, N), jnp.float32)
        return carry

    lax.fori_loop(0, 4 * PATCHES, clear_sums, 0)

    def interact(i, ia, sb, w):
        sa = i * PATCHES + jnp.maximum(ia, 0)
        base = w * WINDOW
        seen = {}

        def b(j, c):
            if (j, c) not in seen:
                seen[j, c] = src[sb, c, pl.ds(base + (PAD + j), 8, stride=STRIDE), :]
            return seen[j, c]

        for u in range(STRIDE):
            a = [tgt[sa, c, pl.ds(base + u, 8, stride=STRIDE), :] for c in range(3)]
            sums = [None] * 4
            for t in range(-BAND, BAND + 1):
                bs = [b(u + t, c) for c in range(4)]
                w_ = jnp.exp2((a[0] * bs[0] + a[1] * bs[1]) + (a[2] * bs[2] + bs[3]))
                terms = [w_ * bs[0], w_ * bs[1], w_ * bs[2], w_]
                sums = [g if s is None else s + g for s, g in zip(sums, terms)]
            rows = pl.ds(pl.multiple_of(base + u * 8, 8), 8)
            for p in range(PATCHES):
                for c in range(4):
                    acc[i * PATCHES + p, c, rows, :] += jnp.where(ia == p, sums[c], 0.0)

    def sources(q, land, k):
        lo, hi, _ = CHUNKS[k]

        def one(p, carry):
            parts = [land[p, c, pl.ds(lo, hi - lo), :].astype(jnp.float32) for c in range(3)]
            for c in range(3):
                src[q * PATCHES + p, c, pl.ds(PAD + lo, hi - lo), :] = parts[c]
            src[q * PATCHES + p, 3, pl.ds(PAD + lo, hi - lo), :] = beta(parts)
            return carry

        lax.fori_loop(0, PATCHES, one, 0)

    def targets(i, k):
        lo, hi, _ = CHUNKS[k]

        def one(p, carry):
            for c in range(3):
                part = x_land[i, p, c, pl.ds(lo, hi - lo), :].astype(jnp.float32)
                tgt[i * PATCHES + p, c, pl.ds(lo, hi - lo), :] = part * (2 * K)
            return carry

        lax.fori_loop(0, PATCHES, one, 0)

    tabs_x = (tab_x1, tab_x2, tab_x3, table)
    run_y = [lax.rem(y + d, YS) for d in (0, 7, 6, 5, 1, 2, 3, 4)]
    run_x = [lax.rem(x + d, XS) for d in (2, 1, 3, 0)]

    def choose(q, i):
        pick[0, q * 4 + i] = tabs_x[i][0, run_y[q] * XS + x]
        pick[1, q * 4 + i] = q * PATCHES + jnp.maximum(tabs_y[q][0, y * XS + run_x[i]], 0)

    def meet(q, k, first, last):
        w0 = CHUNKS[k][2][0]

        def one(n, carry):
            i = first + n // 2
            interact(i, pick[0, q * 4 + i], pick[1, q * 4 + i], w0 + n % 2)
            return carry

        lax.fori_loop(0, 2 * (last - first), one, 0)

    def reduced(i, w, u, p):
        rows = pl.ds(w * WINDOW + u * 8, 8)
        a = [tgt[i * PATCHES + p, c, pl.ds(w * WINDOW + u, 8, stride=STRIDE), :] for c in range(3)]
        level = penalty * jnp.exp2((a[0] * a[0] + a[1] * a[1] + a[2] * a[2]) * (-0.25 / K))
        whole = acc[i * PATCHES + p, 3, rows, :] * (0.5 / K)
        return [level * (a[c] * whole - acc[i * PATCHES + p, c, rows, :]) for c in range(3)]

    def pack(i, w, extra=None):
        def one(p, carry):
            for h in range(STRIDE // 2):
                rows = pl.ds(h * 16, 16)
                pair = [reduced(i, w, 2 * h + e, p) for e in range(2)]
                for c in range(3):
                    f = jnp.concatenate([pair[0][c], pair[1][c]], axis=0)
                    if extra is not None:
                        f = f + extra[p, c, rows, :].astype(jnp.float32)
                    ship[i, w, p, c, rows, :] = f.astype(jnp.bfloat16)
            return carry

        lax.fori_loop(0, PATCHES, one, 0)

    def collect(w):
        def one(p, carry):
            for h in range(STRIDE // 2):
                rows = pl.ds(h * 16, 16)
                pair = [reduced(OWN, w, 2 * h + e, p) for e in range(2)]
                for c in range(3):
                    f = jnp.concatenate([pair[0][c], pair[1][c]], axis=0)
                    f = f + done[0, w, p, c, rows, :].astype(jnp.float32)
                    f = f + done[1, w, p, c, rows, :].astype(jnp.float32)
                    for e in range(2):
                        at_rows = pl.ds(w * WINDOW + 2 * h + e, 8, stride=STRIDE)
                        force[p, c, at_rows, :] = f[e * 8 : e * 8 + 8]
            return carry

        lax.fori_loop(0, PATCHES, one, 0)

    def onward(d, k, p):
        for way, slot, peer in ((1, 0, up), (-1, 3, down)):
            copies.arrived(("y", way * (d - 1), k, p))
            if d < 4:
                cols = columns(k)
                to = slot + d - 1
            else:
                lo, hi = OPPOSITE[k][0 if way == 1 else 1]
                cols = pl.ds(lo, hi - lo)
                to = 6
            copies.start(
                ("y", way * d, k, p),
                y_land.at[slot + d - 2, p, :, cols, :],
                y_land.at[to, p, :, cols, :],
                peer,
            )

    def across(k, p):
        for way, slot, peer in ((1, LEFT, right), (-1, RIGHT, left)):
            copies.arrived(("x", way, k, p))
            lo, hi = HALVES[k][0 if way == 1 else 1]
            cols = pl.ds(lo, hi - lo)
            copies.start(
                ("x", 2 * way, k, p),
                x_land.at[slot, p, :, cols, :],
                x_land.at[TWO, p, :, cols, :],
                peer,
            )

    def base_rows(b, carry):
        r = pl.multiple_of(b * 16, 16)
        lane = lax.broadcasted_iota(jnp.int32, (16, N), 1)
        after = jnp.where(lane == N - 1, 0.0, 0.5)
        before = jnp.where(lane == 0, 0.0, 0.5)
        s = spring[pl.ds(PAD + r, 16), :]
        s_up = 0.5 * (s + spring[pl.ds(PAD + r - 1, 16), :])
        s_down = 0.5 * (s + spring[pl.ds(PAD + r + 1, 16), :])
        s_after = after * (s + pltpu.roll(s, N - 1, 1))
        s_before = before * (s + pltpu.roll(s, 1, 1))
        part = time_step / mass_v[pl.ds(r, 16), :].astype(jnp.float32)
        share[pl.ds(r, 16), :] = part
        for c in range(3):
            v = place[c, pl.ds(PAD + r, 16), :]
            f = s_up * (place[c, pl.ds(PAD + r - 1, 16), :] - v)
            f = f + s_down * (place[c, pl.ds(PAD + r + 1, 16), :] - v)
            f = f + s_after * (pltpu.roll(v, N - 1, 1) - v)
            f = f + s_before * (pltpu.roll(v, 1, 1) - v)
            out[c, 0, pl.ds(r, 16), :] = out[c, 0, pl.ds(r, 16), :] + part * f
        return carry

    copies.arrived(("h", -1))
    copies.arrived(("h", 1))
    for e, row, edge, last in ((0, PAD - 1, PAD, 0), (1, PAD + ROWS, PAD + ROWS - 1, RUNS - 1)):
        for c in range(3):
            place[c, pl.ds(row, 1), :] = jnp.where(
                dev == last, place[c, pl.ds(edge, 1), :], h_land[e, pl.ds(c, 1), :]
            )
        spring[pl.ds(row, 1), :] = h_land[e, pl.ds(3, 1), :]
    loads[4].wait()
    loads[5].wait()
    lax.fori_loop(0, ROWS // 16, base_rows, 0)

    for p in range(PATCHES):
        onward(2, 0, p)
        across(0, p)
    for p in range(PATCHES):
        part = own.at[p, :, columns(1), :]
        copies.start(("x", 1, 1, p), part, x_land.at[LEFT, p, :, columns(1), :], right)
        copies.start(("x", -1, 1, p), part, x_land.at[RIGHT, p, :, columns(1), :], left)
    copies.arrived(("ty", 1))
    copies.start(("ty", 2), tab_y1, tab_y2, up)
    copies.arrived(("ty", -1))
    copies.start(("ty", -2), tab_y4, tab_y5, down)
    copies.arrived(("tx", 1))
    copies.start(("tx", 2), tab_x3, tab_x1, right)
    copies.arrived(("tx", -1))
    targets(RIGHT, 0)
    targets(LEFT, 0)
    sources(1, y_land.at[0], 0)
    sources(4, y_land.at[3], 0)
    for q in (0, 1, 4):
        for i in (RIGHT, LEFT, OWN):
            choose(q, i)
    meet(0, 0, RIGHT, OWN)
    meet(1, 0, RIGHT, OWN + 1)
    meet(4, 0, RIGHT, OWN + 1)

    for p in range(PATCHES):
        onward(3, 0, p)
    copies.arrived(("ty", 2))
    copies.start(("ty", 3), tab_y2, tab_y3, up)
    copies.arrived(("ty", -2))
    copies.start(("ty", -3), tab_y5, tab_y6, down)
    copies.arrived(("tx", 2))
    for p in range(PATCHES):
        onward(2, 1, p)
    for p in range(PATCHES):
        across(1, p)
        for way in (2, -2):
            copies.arrived(("x", way, 0, p))
    targets(TWO, 0)
    sources(2, y_land.at[1], 0)
    sources(5, y_land.at[4], 0)
    for q in (0, 1, 4):
        choose(q, TWO)
    for q in (2, 5):
        for i in range(4):
            choose(q, i)
    for q in (0, 1, 4):
        meet(q, 0, TWO, TWO + 1)
    for q in (2, 5):
        meet(q, 0, 0, 4)

    for p in range(PATCHES):
        onward(4, 0, p)
    copies.arrived(("ty", 3))
    copies.start(("ty", 4), tab_y3, tab_y7, up)
    copies.arrived(("ty", -3))
    sources(3, y_land.at[2], 0)
    sources(6, y_land.at[5], 0)
    for q in (3, 6):
        for i in range(4):
            choose(q, i)
        meet(q, 0, 0, 4)

    for e, way in ((0, -1), (1, 1)):
        copies.arrived(("z", way))
        parts = [z_land[e, c].astype(jnp.float32) for c in range(3)]
        for c in range(3):
            src[8 * PATCHES + e, c, pl.ds(PAD, N), :] = parts[c]
        src[8 * PATCHES + e, 3, pl.ds(PAD, N), :] = beta(parts)

        def one(w, carry, e=e):
            interact(OWN, meets[e], 8 * PATCHES + e, w)
            return carry

        lax.fori_loop(0, N // WINDOW, one, 0)

    for p in range(PATCHES):
        onward(3, 1, p)
    for p in range(PATCHES):
        for way in (2, -2):
            copies.arrived(("x", way, 1, p))
    for i in (TWO, RIGHT, LEFT):
        targets(i, 1)
    meet(0, 1, 0, OWN)

    copies.arrived(("ty", 4))
    for i in range(4):
        choose(7, i)

    def finish(k):
        wa, wb = CHUNKS[k][2]
        for p in range(PATCHES):
            for way in (4, -4):
                copies.arrived(("y", way, k, p))
        sources(7, y_land.at[6], k)
        meet(7, k, TWO, TWO + 1)
        pack(TWO, wa)
        copies.start(("raw", wa), ship.at[TWO, wa], raw.at[wa], right)
        pack(TWO, wb)
        copies.start(("raw", wb), ship.at[TWO, wb], raw.at[wb], left)
        meet(7, k, RIGHT, LEFT + 1)
        pack(RIGHT, wb)
        copies.start(("done", 0, wb), ship.at[RIGHT, wb], done.at[0, wb], right)
        pack(LEFT, wa)
        copies.start(("done", 1, wa), ship.at[LEFT, wa], done.at[1, wa], left)
        meet(7, k, OWN, OWN + 1)

    def relay(k):
        wa, wb = CHUNKS[k][2]
        copies.arrived(("raw", wa))
        pack(RIGHT, wa, raw.at[wa])
        copies.start(("done", 0, wa), ship.at[RIGHT, wa], done.at[0, wa], right)
        copies.arrived(("raw", wb))
        pack(LEFT, wb, raw.at[wb])
        copies.start(("done", 1, wb), ship.at[LEFT, wb], done.at[1, wb], left)

    def gather(k):
        for w in CHUNKS[k][2]:
            copies.arrived(("done", 0, w))
            copies.arrived(("done", 1, w))
            collect(w)

    finish(0)
    sources(1, y_land.at[0], 1)
    sources(4, y_land.at[3], 1)
    meet(1, 1, 0, 4)
    meet(4, 1, 0, 4)
    for p in range(PATCHES):
        onward(4, 1, p)
    relay(0)
    for q, slot in ((2, 1), (5, 4), (3, 2), (6, 5)):
        sources(q, y_land.at[slot], 1)
        meet(q, 1, 0, 4)
    finish(1)
    relay(1)
    gather(0)
    gather(1)

    for p in range(PATCHES):
        rows = pl.ds(p * N, N)
        for c in range(3):
            out[c, 0, rows, :] = out[c, 0, rows, :] + share[rows, :] * force[p, c].T
    copies.sent()


def shards(positions, velocity, node_mass, stiffness, contact_patch, cross_patch):
    table = contact_patch[0]
    cross = cross_patch[0]
    vmem, smem, far = pltpu.VMEM, pltpu.SMEM, pl.ANY
    f32, bf16, i32 = jnp.float32, jnp.bfloat16, jnp.int32
    windows = N // WINDOW
    return pl.pallas_call(
        kernel,
        out_shape=jax.ShapeDtypeStruct(velocity.shape, f32),
        in_specs=[pl.BlockSpec(memory_space=smem)] * 2 + [pl.BlockSpec(memory_space=far)] * 4,
        out_specs=pl.BlockSpec(memory_space=vmem),
        scratch_shapes=[
            vmem((3, ROWS + 2 * PAD, N), f32),
            vmem((ROWS, N), bf16),
            vmem((ROWS, N), bf16),
            vmem((ROWS + 2 * PAD, N), f32),
            vmem((ROWS, N), f32),
            vmem((PATCHES, 3, N, N), bf16),
            vmem((7, PATCHES, 3, N, N), bf16),
            vmem((3, PATCHES, 3, N, N), bf16),
            vmem((8 * PATCHES + 2, 4, N + 2 * PAD, N), f32),
            vmem((4 * PATCHES, 3, N, N), f32),
            vmem((4 * PATCHES, 4, N, N), f32),
            vmem((3, windows, PATCHES, 3, WINDOW, N), bf16),
            vmem((windows, PATCHES, 3, WINDOW, N), bf16),
            vmem((2, windows, PATCHES, 3, WINDOW, N), bf16),
            vmem((PATCHES, 3, N, N), f32),
            vmem((2, 3, N, N), bf16),
            vmem((2, 3, N, N), bf16),
            vmem((2, 8, N), f32),
            vmem((2, 8, N), f32),
        ]
        + [smem((1, RUNS), i32)] * 10
        + [
            smem((2, 32), i32),
            pltpu.SemaphoreType.DMA((6,)),
            pltpu.SemaphoreType.DMA((COPIES,)),
            pltpu.SemaphoreType.DMA((COPIES,)),
        ],
        compiler_params=pltpu.CompilerParams(
            collective_id=0, has_side_effects=True, vmem_limit_bytes=48 * 2**20
        ),
        cost_estimate=pl.CostEstimate(
            flops=600_000_000, bytes_accessed=2_000_000, transcendentals=40_000_000
        ),
    )(table, cross, positions, velocity, node_mass, stiffness)


def solution(mesh):
    return jax.shard_map(
        shards,
        mesh=mesh,
        in_specs=(
            P(None, "seg", "dev", None),
            P(None, "seg", "dev", None),
            P("seg", "dev", None),
            P("seg", "dev", None),
            P("seg", "dev", None),
            P("seg", "dev", None),
        ),
        out_specs=P(None, "seg", "dev", None),
        check_vma=False,
    )
```

time: 161 us -> 62.7 us (0.39)
  the two profiles are of different devices: /device:TPU:24 before, /device:TPU:2 now
where the time goes in v1:
time: 62.7 us; the launch traced here: 62.5 us
  Pallas kernels  57.1 us (91%)
  local copies, waits for them, and re-layouts  5.4 us (9%)
    pallas_call x1, Pallas kernels, shards(): pl.pallas_call(kernel, out_shape=jax.ShapeDtypeStruct(velocity.shape, f32...  57.1 us
    unnamed x13, local copies, waits for them, and re-layouts  5.4 us

profile of v1, /device:TPU:2, one launch (start us, length us, event | category | flops | bytes accessed | tf_op | source)
XLA Modules:
  0.0 62.5 jit_solution(10385359840699791684)
XLA Ops:
  0.0 0.0 copy-start.4
  0.0 0.0 copy-start.5
  0.0 0.7 %copy-done.4 = s32[1,1,32]{2,1,0:T(1,128)S(1)} copy-done((s32[1,1,32]{2,1,0:T(1,128)S(1)}, s32[1,1,32]{2,1,0:T(1,128)}, u32[]{:S(2)}) %copy-start.4) | copy-done | bytes 152
  0.7 0.0 copy-done.5
  0.7 0.0 copy-start
  0.7 1.1 %copy-done = f32[3,1,384,128]{3,2,1,0:T(8,128)S(1)} copy-done((f32[3,1,384,128]{3,2,1,0:T(8,128)S(1)}, f32[3,1,384,128]{3,2,1,0:T(8,128)}, u32[]{:S(2)}) %copy-start) | copy-done | bytes 589848
  1.7 0.0 copy-start.1
  1.7 1.1 %copy-done.1 = f32[3,1,384,128]{3,2,1,0:T(8,128)S(1)} copy-done((f32[3,1,384,128]{3,2,1,0:T(8,128)S(1)}, f32[3,1,384,128]{3,2,1,0:T(8,128)}, u32[]{:S(2)}) %copy-start.1) | copy-done | bytes 589848
  2.8 0.0 copy-start.2
  2.8 0.9 %copy-done.2 = bf16[1,384,128]{2,1,0:T(8,128)(2,1)S(1)} copy-done((bf16[1,384,128]{2,1,0:T(8,128)(2,1)S(1)}, bf16[1,384,128]{2,1,0:T(8,128)(2,1)}, u32[]{:S(2)}) %copy-start.2) | copy-done | bytes 98328
  3.7 0.0 copy-start.3
  3.7 0.9 %copy-done.3 = bf16[1,384,128]{2,1,0:T(8,128)(2,1)S(1)} copy-done((bf16[1,384,128]{2,1,0:T(8,128)(2,1)S(1)}, bf16[1,384,128]{2,1,0:T(8,128)(2,1)}, u32[]{:S(2)}) %copy-start.3) | copy-done | bytes 98328
  4.6 57.1 %shard_map.64 = f32[3,1,384,128]{3,2,1,0:T(8,128)S(1)} custom-call(s32[1,32]{1,0:T(1,128)S(1)} %bitcast.2, s32[1,2]{1,0:T(1,128)S(1)} %bitcast.3, f32[3,1,384,128]{3,2,1,0:T(8,128)S(1)} %copy-done, f32[3,1,384,128]{3,2,1,0:T(8,128)S(1)} %copy-done.1, bf16[1,384,128]{2,1,0:T(8,128)(2,1)S(1)} %copy-done.2, bf16[1,384,128]{2,1,0:T(8,128)(2,1)S(1)} %copy-done.3), custom_call_target="tpu_custom_call" | custom-call | flops 600000000 | bytes 2000000 | tf_op jit(solution)/shard_map/pallas_call | solution.py:489
  61.7 0.8 %copy.8 = f32[3,1,384,128]{3,2,1,0:T(8,128)} copy(f32[3,1,384,128]{3,2,1,0:T(8,128)S(1)} %shard_map.64) | data formatting | bytes 1179648
Async XLA Ops:
  0.0 0.7 %copy-start.4 = (s32[1,1,32]{2,1,0:T(1,128)S(1)}, s32[1,1,32]{2,1,0:T(1,128)}, u32[]{:S(2)}) copy-start(s32[1,1,32]{2,1,0:T(1,128)} %param.10) | copy-start | bytes 388
  0.0 0.7 %copy-start.5 = (s32[1,1,2]{2,1,0:T(1,128)S(1)}, s32[1,1,2]{2,1,0:T(1,128)}, u32[]{:S(2)}) copy-start(s32[1,1,2]{2,1,0:T(1,128)} %param.11) | copy-start | bytes 28
  0.7 1.1 %copy-start = (f32[3,1,384,128]{3,2,1,0:T(8,128)S(1)}, f32[3,1,384,128]{3,2,1,0:T(8,128)}, u32[]{:S(2)}) copy-start(f32[3,1,384,128]{3,2,1,0:T(8,128)} %pos.1) | copy-start | bytes 1769476
  1.7 1.1 %copy-start.1 = (f32[3,1,384,128]{3,2,1,0:T(8,128)S(1)}, f32[3,1,384,128]{3,2,1,0:T(8,128)}, u32[]{:S(2)}) copy-start(f32[3,1,384,128]{3,2,1,0:T(8,128)} %vel.1) | copy-start | bytes 1769476
  2.8 0.9 %copy-start.2 = (bf16[1,384,128]{2,1,0:T(8,128)(2,1)S(1)}, bf16[1,384,128]{2,1,0:T(8,128)(2,1)}, u32[]{:S(2)}) copy-start(bf16[1,384,128]{2,1,0:T(8,128)(2,1)} %mass.1) | copy-start | bytes 294916
  3.7 0.9 %copy-start.3 = (bf16[1,384,128]{2,1,0:T(8,128)(2,1)S(1)}, bf16[1,384,128]{2,1,0:T(8,128)(2,1)}, u32[]{:S(2)}) copy-start(bf16[1,384,128]{2,1,0:T(8,128)(2,1)} %stiff.1) | copy-start | bytes 294916

commit v2 on v1

v2 whole, which is shorter than its diff:
```python
import functools
import math

import jax
import jax.numpy as jnp
from jax import lax
from jax.experimental import pallas as pl
from jax.experimental.pallas import tpu as pltpu
from jax.sharding import PartitionSpec as P

RUNS = 32
XS = 4
YS = 8
PATCHES = 3
N = 128
BAND = 4
PAD = 8
STRIDE = 4
WINDOW = 8 * STRIDE
ROWS = PATCHES * N

penalty = 1.5
reach_sq = 4.0
time_step = 0.2
K = math.log2(math.e) / reach_sq
FAR = -1.0e4

CHUNKS = (
    (0, 48, (0,)),
    (48, 80, (1,)),
    (80, 112, (2,)),
    (112, 128, (3,)),
)

HALVES = (
    ((0, 32), (32, 48)),
    ((48, 64), (64, 80)),
    ((80, 96), (96, 112)),
    ((112, 112), (112, 128)),
)

ORDER = (
    ('y', 1, 0),
    ('y', 1, 1),
    ('y', 1, 2),
    ('y', 1, 3),
    ('x', 1, 0),
    ('x', 1, 1),
    ('x', 1, 2),
    ('x', 1, 3),
    ('z',),
    ('h',),
    ('y', 2, 0),
    ('s', 1, 0),
    ('x', 2, 0),
    ('t', 1, 0),
    ('m', 0, 0, 1),
    ('m', 1, 0, 1),
    ('b',),
    ('y', 2, 1),
    ('x', 2, 1),
    ('s', 1, 1),
    ('t', 1, 1),
    ('m', 0, 1, 1),
    ('m', 1, 1, 1),
    ('y', 2, 2),
    ('x', 2, 2),
    ('t', 1, 2),
    ('y', 2, 3),
    ('s', 1, 2),
    ('s', 1, 3),
    ('m', 0, 2, 1),
    ('m', 1, 2, 1),
    ('x', 2, 3),
    ('t', 1, 3),
    ('m', 0, 3, 1),
    ('m', 1, 3, 1),
    ('t', 2, 0),
    ('m', 0, 0, 0),
    ('m', 1, 0, 0),
    ('w',),
    ('y', 3, 0),
    ('s', 2, 0),
    ('t', 2, 1),
    ('m', 2, 0, 2),
    ('y', 3, 1),
    ('s', 2, 1),
    ('t', 2, 2),
    ('t', 2, 3),
    ('m', 0, 1, 0),
    ('m', 1, 1, 0),
    ('m', 2, 1, 2),
    ('m', 0, 2, 0),
    ('m', 1, 2, 0),
    ('m', 0, 3, 0),
    ('y', 3, 2),
    ('s', 2, 2),
    ('m', 2, 2, 2),
    ('y', 3, 3),
    ('s', 2, 3),
    ('m', 1, 3, 0),
    ('m', 2, 3, 2),
    ('y', 4, 0),
    ('s', 3, 0),
    ('m', 3, 0, 2),
    ('y', 4, 1),
    ('s', 3, 1),
    ('m', 3, 1, 2),
    ('y', 4, 2),
    ('s', 3, 2),
    ('m', 3, 2, 2),
    ('y', 4, 3),
    ('s', 3, 3),
    ('m', 3, 3, 2),
    ('s', 4, 0),
    ('m', 4, 0, 0),
    ('r', 0, 0),
    ('m', 4, 0, 1),
    ('r', 1, 0),
    ('s', 4, 1),
    ('m', 4, 0, 3),
    ('m', 4, 1, 0),
    ('r', 0, 1),
    ('m', 4, 1, 1),
    ('r', 1, 1),
    ('s', 4, 2),
    ('m', 4, 1, 3),
    ('m', 4, 2, 0),
    ('r', 0, 2),
    ('s', 4, 3),
    ('m', 4, 2, 1),
    ('r', 1, 2),
    ('m', 4, 2, 3),
    ('m', 4, 3, 0),
    ('r', 0, 3),
    ('m', 4, 3, 1),
    ('r', 1, 3),
    ('m', 4, 3, 3),
    ('r', 2, 0),
    ('r', 2, 1),
    ('r', 2, 2),
    ('r', 2, 3),
    ('c', 0),
    ('c', 1),
    ('c', 2),
    ('c', 3),
)

TWO, RIGHT, LEFT, OWN = range(4)
MEET = {0: (TWO, TWO + 1), 1: (RIGHT, OWN + 1), 2: (TWO, OWN + 1), 3: (OWN, OWN + 1)}
COPIES = 160


class Copies:
    def __init__(self, send_sem, recv_sem):
        self.send_sem, self.recv_sem = send_sem, recv_sem
        self.made = {}
        self.seen = set()

    def start(self, name, src, dst, device):
        n = len(self.made)
        copy = pltpu.make_async_remote_copy(
            src_ref=src,
            dst_ref=dst,
            send_sem=self.send_sem.at[n],
            recv_sem=self.recv_sem.at[n],
            device_id=device,
            device_id_type=pl.DeviceIdType.MESH,
        )
        copy.start()
        self.made[name] = copy

    def arrived(self, *names):
        for name in names:
            if name in self.made and name not in self.seen:
                self.made[name].wait_recv()
                self.seen.add(name)

    def sent(self):
        for copy in self.made.values():
            copy.wait_send()


def kernel(
    contact, facing, pos, vel, mass, stiff, out,
    place, mass_v, stiff_v, spring, share, own, y_land, x_land, src, tgt, acc,
    ship, raw, done, force, z_send, z_land, h_send, h_land,
    tab_y1, tab_y2, tab_y3, tab_y4, tab_y5, tab_y6, tab_y7, tab_x1, tab_x2, tab_x3, table, cross, pick,
    local_sem, send_sem, recv_sem,
):
    seg = lax.axis_index("seg")
    dev = lax.axis_index("dev")
    segs = lax.axis_size("seg")
    y = dev // XS
    x = dev % XS

    def at(dy, dx):
        return (seg, lax.rem(y + dy, YS) * XS + lax.rem(x + dx, XS))

    up, down = at(1, 0), at(YS - 1, 0)
    right, left = at(0, 1), at(0, XS - 1)
    seg_next, seg_prev = (lax.rem(seg + 1, segs), dev), (lax.rem(seg + segs - 1, segs), dev)
    dev_next, dev_prev = (seg, lax.rem(dev + 1, RUNS)), (seg, lax.rem(dev + RUNS - 1, RUNS))

    barrier = pltpu.get_barrier_semaphore()
    peers = (up, down, right, left, seg_next, seg_prev, dev_next, dev_prev)
    for peer in peers:
        pl.semaphore_signal(barrier, inc=1, device_id=peer, device_id_type=pl.DeviceIdType.MESH)

    loads = []
    for p in range(PATCHES):
        loads.append(
            pltpu.make_async_copy(
                pos.at[:, 0, pl.ds(p * N, N), :],
                place.at[:, pl.ds(PAD + p * N, N), :],
                local_sem.at[p],
            )
        )
    loads.append(pltpu.make_async_copy(stiff.at[0], stiff_v, local_sem.at[3]))
    loads.append(pltpu.make_async_copy(mass.at[0], mass_v, local_sem.at[4]))
    loads.append(pltpu.make_async_copy(vel, out, local_sem.at[5]))
    loads.append(pltpu.make_async_copy(contact.at[0], table, local_sem.at[6]))
    loads.append(pltpu.make_async_copy(facing.at[0], cross, local_sem.at[7]))
    for load in loads:
        load.start()

    def clear(n, carry):
        for c in range(4):
            edge = jnp.full((PAD, N), FAR if c == 3 else 0.0, jnp.float32)
            src[n, c, pl.ds(0, PAD), :] = edge
            src[n, c, pl.ds(PAD + N, PAD), :] = edge
        return carry

    lax.fori_loop(0, 8 * PATCHES + 2, clear, 0)

    def clear_sums(n, carry):
        for c in range(4):
            acc[n, c] = jnp.zeros((N, N), jnp.float32)
        return carry

    copies = Copies(send_sem, recv_sem)

    def columns(k):
        lo, hi, _ = CHUNKS[k]
        return pl.ds(lo, hi - lo)

    def beta(xs):
        return -K * (xs[0] * xs[0] + xs[1] * xs[1] + xs[2] * xs[2])

    for p in range(PATCHES):
        loads[p].wait()
    for p in range(PATCHES):
        parts = []
        for c in range(3):
            turned = place[c, pl.ds(PAD + p * N, N), :].T.astype(jnp.bfloat16)
            own[p, c] = turned
            parts.append(turned.astype(jnp.float32))
        for c in range(3):
            src[p, c, pl.ds(PAD, N), :] = parts[c]
            tgt[OWN * PATCHES + p, c] = parts[c] * (2 * K)
        src[p, 3, pl.ds(PAD, N), :] = beta(parts)
    loads[3].wait()
    for e, row in enumerate((0, ROWS - 1)):
        first = row // 16 * 16
        for c in range(3):
            h_send[e, pl.ds(c, 1), :] = place[c, pl.ds(PAD + row, 1), :]
        edge = stiff_v[pl.ds(first, 16), :].astype(jnp.float32)
        h_send[e, pl.ds(3, 1), :] = edge[row - first : row - first + 1]
        h_send[e, pl.ds(4, 4), :] = jnp.zeros((4, N), jnp.float32)

    loads[6].wait()
    loads[7].wait()
    pl.semaphore_wait(barrier, len(peers))
    tabs_y = (table, tab_y1, tab_y2, tab_y3, tab_y4, tab_y5, tab_y6, tab_y7)
    copies.start(("ty", 1), table, tab_y1, up)
    copies.start(("ty", -1), table, tab_y4, down)
    copies.start(("tx", 1), table, tab_x3, right)
    copies.start(("tx", -1), table, tab_x2, left)
    copies.start(("h", -1), h_send.at[0], h_land.at[1], dev_prev)
    copies.start(("h", 1), h_send.at[1], h_land.at[0], dev_next)

    def interact(i, ia, sb, w):
        sa = i * PATCHES + jnp.maximum(ia, 0)
        base = w * WINDOW
        seen = {}

        def b(j, c):
            if (j, c) not in seen:
                seen[j, c] = src[sb, c, pl.ds(base + (PAD + j), 8, stride=STRIDE), :]
            return seen[j, c]

        for u in range(STRIDE):
            a = [tgt[sa, c, pl.ds(base + u, 8, stride=STRIDE), :] for c in range(3)]
            sums = [None] * 4
            for t in range(-BAND, BAND + 1):
                bs = [b(u + t, c) for c in range(4)]
                w_ = jnp.exp2((a[0] * bs[0] + a[1] * bs[1]) + (a[2] * bs[2] + bs[3]))
                terms = [w_ * bs[0], w_ * bs[1], w_ * bs[2], w_]
                sums = [g if s is None else s + g for s, g in zip(sums, terms)]
            rows = pl.ds(pl.multiple_of(base + u * 8, 8), 8)
            for p in range(PATCHES):
                for c in range(4):
                    acc[i * PATCHES + p, c, rows, :] += jnp.where(ia == p, sums[c], 0.0)

    def sources(q, land, k):
        lo, hi, _ = CHUNKS[k]

        def one(p, carry):
            parts = [land[p, c, pl.ds(lo, hi - lo), :].astype(jnp.float32) for c in range(3)]
            for c in range(3):
                src[q * PATCHES + p, c, pl.ds(PAD + lo, hi - lo), :] = parts[c]
            src[q * PATCHES + p, 3, pl.ds(PAD + lo, hi - lo), :] = beta(parts)
            return carry

        lax.fori_loop(0, PATCHES, one, 0)

    def targets(i, k):
        lo, hi, _ = CHUNKS[k]

        def one(p, carry):
            for c in range(3):
                part = x_land[i, p, c, pl.ds(lo, hi - lo), :].astype(jnp.float32)
                tgt[i * PATCHES + p, c, pl.ds(lo, hi - lo), :] = part * (2 * K)
            return carry

        lax.fori_loop(0, PATCHES, one, 0)

    tabs_x = (tab_x1, tab_x2, tab_x3, table)
    run_y = [lax.rem(y + d, YS) for d in (0, 7, 6, 5, 1, 2, 3, 4)]
    run_x = [lax.rem(x + d, XS) for d in (2, 1, 3, 0)]

    def choose(q, i):
        pick[0, q * 4 + i] = tabs_x[i][0, run_y[q] * XS + x]
        pick[1, q * 4 + i] = q * PATCHES + jnp.maximum(tabs_y[q][0, y * XS + run_x[i]], 0)

    def meet(q, runs, k, group):
        first, last = MEET[group]
        if group == 1 and q in (0, 7):
            last = OWN
        windows = CHUNKS[k][2]
        for n in range(runs):
            for i in range(first, last):
                choose(q + 3 * n, i)

        def one(n, carry):
            i = first + n // len(windows) % (last - first)
            at_q = q + 3 * (n // (len(windows) * (last - first)))
            interact(i, pick[0, at_q * 4 + i], pick[1, at_q * 4 + i], windows[0] + n % len(windows))
            return carry

        lax.fori_loop(0, runs * (last - first) * len(windows), one, 0)

    def reduced(i, w, u, p):
        rows = pl.ds(w * WINDOW + u * 8, 8)
        a = [tgt[i * PATCHES + p, c, pl.ds(w * WINDOW + u, 8, stride=STRIDE), :] for c in range(3)]
        level = penalty * jnp.exp2((a[0] * a[0] + a[1] * a[1] + a[2] * a[2]) * (-0.25 / K))
        whole = acc[i * PATCHES + p, 3, rows, :] * (0.5 / K)
        return [level * (a[c] * whole - acc[i * PATCHES + p, c, rows, :]) for c in range(3)]

    def pack(i, w, h, extra=None):
        def one(p, carry):
            pair = [reduced(i, w, 2 * h + e, p) for e in range(2)]
            for c in range(3):
                f = jnp.concatenate([pair[0][c], pair[1][c]], axis=0)
                if extra is not None:
                    f = f + extra[p, c].astype(jnp.float32)
                ship[i, w, h, p, c] = f.astype(jnp.bfloat16)
            return carry

        lax.fori_loop(0, PATCHES, one, 0)

    def collect(w):
        def one(p, carry):
            for h in range(STRIDE // 2):
                pair = [reduced(OWN, w, 2 * h + e, p) for e in range(2)]
                for c in range(3):
                    f = jnp.concatenate([pair[0][c], pair[1][c]], axis=0)
                    f = f + done[0, w, h, p, c].astype(jnp.float32)
                    f = f + done[1, w, h, p, c].astype(jnp.float32)
                    for e in range(2):
                        at_rows = pl.ds(w * WINDOW + 2 * h + e, 8, stride=STRIDE)
                        force[p, c, at_rows, :] = f[e * 8 : e * 8 + 8]
            return carry

        lax.fori_loop(0, PATCHES, one, 0)

    ways = ((1, 0, up), (-1, 3, down))

    def along(d, k):
        for way, slot, peer in ways:
            copies.arrived(("y", way * (d - 1), k))
            lo, hi, _ = CHUNKS[k]
            if d == 4:
                lo, hi = HALVES[k][0 if way == 1 else 1]
            if lo == hi:
                continue
            cols = pl.ds(lo, hi - lo)
            to = 6 if d == 4 else slot + d - 1
            part = own.at[:, :, cols, :] if d == 1 else y_land.at[slot + d - 2, :, :, cols, :]
            copies.start(("y", way * d, k), part, y_land.at[to, :, :, cols, :], peer)
        if k == 0 and d > 1:
            for way, slot, peer in ways[: 1 if d == 4 else 2]:
                copies.arrived(("ty", way * (d - 1)))
                to = 7 if d == 4 else slot + d
                copies.start(("ty", way * d), tabs_y[slot + d - 1], tabs_y[to], peer)

    def across(d, k):
        for n, (way, slot, peer) in enumerate(((1, LEFT, right), (-1, RIGHT, left))):
            lo, hi, _ = CHUNKS[k]
            if d == 2:
                copies.arrived(("x", way, k))
                lo, hi = HALVES[k][n]
            if lo == hi:
                continue
            cols = pl.ds(lo, hi - lo)
            part = own.at[:, :, cols, :] if d == 1 else x_land.at[slot, :, :, cols, :]
            to = slot if d == 1 else TWO
            copies.start(("x", way * d, k), part, x_land.at[to, :, :, cols, :], peer)
        if k == 0 and d == 2:
            copies.arrived(("tx", 1))
            copies.start(("tx", 2), tab_x3, tab_x1, right)

    def reduce_stage(stage, k):
        for w in CHUNKS[k][2]:
            for h, i, peer in ((0, RIGHT, right), (1, LEFT, left)):
                if stage == 0:
                    pack(TWO, w, h)
                    copies.start(("raw", w, h), ship.at[TWO, w, h], raw.at[w, h], peer)
                elif stage == 1:
                    pack(i, w, 1 - h)
                    copies.start(("done", w, h, 1 - h), ship.at[i, w, 1 - h], done.at[h, w, 1 - h], peer)
                else:
                    copies.arrived(("raw", w, h))
                    pack(i, w, h, raw.at[w, h])
                    copies.start(("done", w, h, h), ship.at[i, w, h], done.at[h, w, h], peer)

    def base_rows(b, carry):
        r = pl.multiple_of(b * 16, 16)
        lane = lax.broadcasted_iota(jnp.int32, (16, N), 1)
        after = jnp.where(lane == N - 1, 0.0, 0.5)
        before = jnp.where(lane == 0, 0.0, 0.5)
        s = spring[pl.ds(PAD + r, 16), :]
        s_up = 0.5 * (s + spring[pl.ds(PAD + r - 1, 16), :])
        s_down = 0.5 * (s + spring[pl.ds(PAD + r + 1, 16), :])
        s_after = after * (s + pltpu.roll(s, N - 1, 1))
        s_before = before * (s + pltpu.roll(s, 1, 1))
        part = time_step / mass_v[pl.ds(r, 16), :].astype(jnp.float32)
        share[pl.ds(r, 16), :] = part
        for c in range(3):
            v = place[c, pl.ds(PAD + r, 16), :]
            f = s_up * (place[c, pl.ds(PAD + r - 1, 16), :] - v)
            f = f + s_down * (place[c, pl.ds(PAD + r + 1, 16), :] - v)
            f = f + s_after * (pltpu.roll(v, N - 1, 1) - v)
            f = f + s_before * (pltpu.roll(v, 1, 1) - v)
            out[c, 0, pl.ds(r, 16), :] = out[c, 0, pl.ds(r, 16), :] + part * f
        return carry

    def halo():
        for b in range(ROWS // WINDOW):
            rows = pl.ds(b * WINDOW, WINDOW)
            spring[pl.ds(PAD + b * WINDOW, WINDOW), :] = stiff_v[rows, :].astype(jnp.float32)
        copies.arrived(("h", -1), ("h", 1))
        for e, row, edge, last in ((0, PAD - 1, PAD, 0), (1, PAD + ROWS, PAD + ROWS - 1, RUNS - 1)):
            for c in range(3):
                place[c, pl.ds(row, 1), :] = jnp.where(
                    dev == last, place[c, pl.ds(edge, 1), :], h_land[e, pl.ds(c, 1), :]
                )
            spring[pl.ds(row, 1), :] = h_land[e, pl.ds(3, 1), :]
        loads[4].wait()
        loads[5].wait()
        lax.fori_loop(0, ROWS // 16, base_rows, 0)

    meets = [cross[0, 0], cross[0, 1]]

    def send_cross():
        for c in range(3):
            z_send[0, c] = own[meets[0], c]
            z_send[1, c] = own[meets[1], c]
        copies.start(("z", 1), z_send.at[0], z_land.at[1], seg_next)
        copies.start(("z", -1), z_send.at[1], z_land.at[0], seg_prev)

    def meet_cross():
        for e, way in ((0, -1), (1, 1)):
            copies.arrived(("z", way))
            parts = [z_land[e, c].astype(jnp.float32) for c in range(3)]
            for c in range(3):
                src[8 * PATCHES + e, c, pl.ds(PAD, N), :] = parts[c]
            src[8 * PATCHES + e, 3, pl.ds(PAD, N), :] = beta(parts)

        def one(n, carry):
            e = n // (N // WINDOW)
            ia = jnp.where(e == 0, meets[0], meets[1])
            interact(OWN, ia, 8 * PATCHES + e, n % (N // WINDOW))
            return carry

        lax.fori_loop(0, 2 * N // WINDOW, one, 0)

    for kind, *step in ORDER:
        if kind == "y":
            along(*step)
        elif kind == "x":
            across(*step)
        elif kind == "t":
            way, k = step
            if way == 1:
                copies.arrived(("x", 1, k), ("x", -1, k))
                targets(RIGHT, k)
                targets(LEFT, k)
            else:
                copies.arrived(("x", 2, k), ("x", -2, k))
                targets(TWO, k)
        elif kind == "s":
            d, k = step
            copies.arrived(("y", d, k), ("y", -d, k))
            if d == 4:
                sources(7, y_land.at[6], k)
            else:
                sources(d, y_land.at[d - 1], k)
                sources(d + 3, y_land.at[d + 2], k)
        elif kind == "m":
            d, k, group = step
            if k == 0:
                copies.arrived(("ty", d), ("ty", -d), ("tx", 1), ("tx", -1))
                if group in (0, 2):
                    copies.arrived(("tx", 2))
            meet(7 if d == 4 else d, 1 if d in (0, 4) else 2, k, group)
        elif kind == "r":
            reduce_stage(*step)
        elif kind == "c":
            (k,) = step
            for w in CHUNKS[k][2]:
                copies.arrived(*((("done", w, h, e)) for h in range(2) for e in range(2)))
                collect(w)
        elif kind == "h":
            lax.fori_loop(0, 4 * PATCHES, clear_sums, 0)
        elif kind == "b":
            halo()
        elif kind == "z":
            send_cross()
        elif kind == "w":
            meet_cross()

    for p in range(PATCHES):
        rows = pl.ds(p * N, N)
        for c in range(3):
            out[c, 0, rows, :] = out[c, 0, rows, :] + share[rows, :] * force[p, c].T
    copies.sent()


def shards(positions, velocity, node_mass, stiffness, contact_patch, cross_patch):
    vmem, smem = pltpu.VMEM, pltpu.SMEM
    f32, bf16, i32 = jnp.float32, jnp.bfloat16, jnp.int32
    windows = N // WINDOW
    return pl.pallas_call(
        kernel,
        out_shape=jax.ShapeDtypeStruct(velocity.shape, f32),
        in_specs=[pl.BlockSpec(memory_space=pltpu.HBM)] * 6,
        out_specs=pl.BlockSpec(memory_space=vmem),
        scratch_shapes=[
            vmem((3, ROWS + 2 * PAD, N), f32),
            vmem((ROWS, N), bf16),
            vmem((ROWS, N), bf16),
            vmem((ROWS + 2 * PAD, N), f32),
            vmem((ROWS, N), f32),
            vmem((PATCHES, 3, N, N), bf16),
            vmem((7, PATCHES, 3, N, N), bf16),
            vmem((3, PATCHES, 3, N, N), bf16),
            vmem((8 * PATCHES + 2, 4, N + 2 * PAD, N), f32),
            vmem((4 * PATCHES, 3, N, N), f32),
            vmem((4 * PATCHES, 4, N, N), f32),
            vmem((3, windows, 2, PATCHES, 3, WINDOW // 2, N), bf16),
            vmem((windows, 2, PATCHES, 3, WINDOW // 2, N), bf16),
            vmem((2, windows, 2, PATCHES, 3, WINDOW // 2, N), bf16),
            vmem((PATCHES, 3, N, N), f32),
            vmem((2, 3, N, N), bf16),
            vmem((2, 3, N, N), bf16),
            vmem((2, 8, N), f32),
            vmem((2, 8, N), f32),
        ]
        + [smem((1, RUNS), i32)] * 11
        + [
            smem((1, 2), i32),
            smem((2, 32), i32),
            pltpu.SemaphoreType.DMA((8,)),
            pltpu.SemaphoreType.DMA((COPIES,)),
            pltpu.SemaphoreType.DMA((COPIES,)),
        ],
        compiler_params=pltpu.CompilerParams(
            collective_id=0, has_side_effects=True, vmem_limit_bytes=60 * 2**20
        ),
        cost_estimate=pl.CostEstimate(
            flops=600_000_000, bytes_accessed=2_000_000, transcendentals=40_000_000
        ),
    )(contact_patch, cross_patch, positions, velocity, node_mass, stiffness)


def solution(mesh):
    return jax.shard_map(
        shards,
        mesh=mesh,
        in_specs=(
            P(None, "seg", "dev", None),
            P(None, "seg", "dev", None),
            P("seg", "dev", None),
            P("seg", "dev", None),
            P("seg", "dev", None),
            P("seg", "dev", None),
        ),
        out_specs=P(None, "seg", "dev", None),
        check_vma=False,
    )
```

time: 62.7 us -> 49 us (0.78)
  the two profiles are of different devices: /device:TPU:2 before, /device:TPU:8 now
where the time goes in v2:
time: 49 us; the launch traced here: 48.8 us
  Pallas kernels  46.9 us (96%)
  local copies, waits for them, and re-layouts  1.92 us (4%)
    pallas_call x1, Pallas kernels, shards(): pl.pallas_call(kernel, out_shape=jax.ShapeDtypeStruct(velocity.shape, f32...  46.9 us
    unnamed x1, local copies, waits for them, and re-layouts  1.92 us

profile of v2, /device:TPU:8, one launch (start us, length us, event | category | flops | bytes accessed | tf_op | source)
XLA Modules:
  0.0 48.8 jit_solution(4679009286550299795)
XLA Ops:
  0.0 46.9 %shard_map.64 = f32[3,1,384,128]{3,2,1,0:T(8,128)} custom-call(s32[1,1,32]{2,1,0:T(1,128)} %contact.1, s32[1,1,2]{2,1,0:T(1,128)} %facing.1, f32[3,1,384,128]{3,2,1,0:T(8,128)} %pos.1, f32[3,1,384,128]{3,2,1,0:T(8,128)} %vel.1, bf16[1,384,128]{2,1,0:T(8,128)(2,1)} %mass.1, bf16[1,384,128]{2,1,0:T(8,128)(2,1)} %stiff.1), custom_call_target="tpu_custom_call" | custom-call | flops 600000000 | bytes 2000000 | tf_op jit(solution)/shard_map/pallas_call | solution.py:554
  46.9 1.9 %copy.8 = f32[3,1,384,128]{3,2,1,0:T(8,128)} copy(f32[3,1,384,128]{3,2,1,0:T(8,128)} %shard_map.64) | data formatting | bytes 1179648
